TPU v7x, 256 devices: a whole 4x4x8 slice. The times are simulated.
256 devices in a mesh: pipe: 8 (over y, core), feat: 32 (over x, z).
Axes of the slice: x: 4, y: 4, z: 8, core: 2. Of those that a mesh axis runs over, the one named last changes fastest.
Arguments:
- grad_out: bfloat16 [512, 8192], P(None, 'feat'), may hold values from -6 to 6
- saved_input: bfloat16 [8, 512, 8192], P('pipe', None, 'feat'), may hold values from -6 to 6
- saved_first: bfloat16 [8, 512, 8192], P('pipe', None, 'feat'), may hold values from -6 to 6
- saved_pre: bfloat16 [8, 512, 8192], P('pipe', None, 'feat'), may hold values from -6 to 6
- saved_second: bfloat16 [8, 512, 8192], P('pipe', None, 'feat'), may hold values from -6 to 6
- right_one: bfloat16 [8, 64, 128, 128], P('pipe', 'feat'), may hold values from -0.5 to 0.5
- left_one: bfloat16 [8, 64, 128, 128], P('pipe', 'feat'), may hold values from -0.5 to 0.5
- right_two: bfloat16 [8, 64, 128, 128], P('pipe', 'feat'), may hold values from -0.5 to 0.5
- left_two: bfloat16 [8, 64, 128, 128], P('pipe', 'feat'), may hold values from -0.5 to 0.5
Outputs:
- grad_input: bfloat16 [8, 512, 8192], P('pipe', None, 'feat')
- grad_right_one: bfloat16 [8, 64, 128, 128], P('pipe', 'feat')
- grad_left_one: bfloat16 [8, 64, 128, 128], P('pipe', 'feat')
- grad_right_two: bfloat16 [8, 64, 128, 128], P('pipe', 'feat')
- grad_left_two: bfloat16 [8, 64, 128, 128], P('pipe', 'feat')
All inputs are finite; a program needn't handle non-finite values.
Results may differ from a plain program's by a relative error of at most 0.034.
Values may be sent and summed in bfloat16 or wider, within the bound.
No kernel may reach another device: no remote copies, remote signals or barrier semaphores. Data moves between devices by JAX's collectives and lax.ppermute only.
A program may use at most 64 MiB of HBM per device.

v0:
```python
import jax
import jax.numpy as jnp
from jax import lax
from jax.sharding import PartitionSpec as P

BS = 128
H = 2


def passed_along(block, axis, distance):
    devices = range(lax.axis_size(axis))
    route = [(i - distance, i) for i in devices if i - distance in devices]
    return lax.ppermute(block, axis, route)


def to_wire(v, nfeat):
    t = v.shape[0]
    nloc = v.shape[1] // BS
    return v.T.reshape(nloc, H, nfeat, nloc, t)


def from_wire(w):
    t = w.shape[4]
    return w.transpose(3, 1, 2, 0, 4).reshape(-1, t).T


def apply_transposed(v, weight):
    t = v.shape[0]
    out = jnp.einsum(
        "tkj,kij->tki", v.reshape(t, -1, BS), weight, preferred_element_type=jnp.float32
    )
    return out.reshape(t, -1)


def weight_grad(left, right):
    t = left.shape[0]
    return jnp.einsum(
        "tki,tkj->kij",
        left.reshape(t, -1, BS),
        right.reshape(t, -1, BS),
        preferred_element_type=jnp.float32,
    )


def layer_backward(dy, x_rows, first_rows, pre_rows, second_rows, weights):
    right_a, left_a, right_b, left_b = weights
    nfeat = lax.axis_size("feat")
    out2 = from_wire(
        lax.all_to_all(to_wire(dy, nfeat), "feat", split_axis=2, concat_axis=2, tiled=True)
    )
    grad_l2 = weight_grad(second_rows, out2)
    back2 = apply_transposed(out2, left_b).astype(jnp.bfloat16)
    mid2 = from_wire(
        lax.all_to_all(to_wire(back2, nfeat), "feat", split_axis=2, concat_axis=2, tiled=True)
    )
    z = pre_rows.astype(jnp.float32)
    cdf = 0.5 * (1.0 + jax.scipy.special.erf(z * 0.7071067811865476))
    act = (z * cdf).astype(jnp.bfloat16)
    grad_r2 = weight_grad(act, mid2)
    slope = cdf + z * jnp.exp(-0.5 * z * z) * 0.3989422804014327
    pre_grad = (apply_transposed(mid2, right_b) * slope).astype(jnp.bfloat16)
    out1 = from_wire(
        lax.all_to_all(to_wire(pre_grad, nfeat), "feat", split_axis=2, concat_axis=2, tiled=True)
    )
    grad_l1 = weight_grad(first_rows, out1)
    back1 = apply_transposed(out1, left_a).astype(jnp.bfloat16)
    mid1 = from_wire(
        lax.all_to_all(to_wire(back1, nfeat), "feat", split_axis=2, concat_axis=2, tiled=True)
    )
    grad_r1 = weight_grad(x_rows, mid1)
    grad_x = (dy.astype(jnp.float32) + apply_transposed(mid1, right_a)).astype(jnp.bfloat16)
    return (grad_x, (grad_r1, grad_l1, grad_r2, grad_l2))


def shards(
    grad_out,
    saved_input,
    saved_first,
    saved_pre,
    saved_second,
    right_one,
    left_one,
    right_two,
    left_two,
):
    section = lax.axis_index("pipe")
    nsec = lax.axis_size("pipe")
    is_last = section == nsec - 1
    weights = (right_one[0], left_one[0], right_two[0], left_two[0])
    acts = (saved_input[0], saved_first[0], saved_pre[0], saved_second[0])
    totals = tuple((jnp.zeros(w.shape, jnp.float32) for w in weights))
    grad_x_all = jnp.zeros(grad_out.shape, jnp.bfloat16)
    carried = jnp.where(is_last, grad_out, jnp.zeros_like(grad_out))
    for turn in range(nsec):
        grad_x, grads = layer_backward(carried, acts[0], acts[1], acts[2], acts[3], weights)
        active = turn == nsec - 1 - section
        grad_x_all = jnp.where(active, grad_x, grad_x_all)
        totals = tuple((jnp.where(active, g, total) for g, total in zip(grads, totals)))
        if turn < nsec - 1:
            carried = passed_along(grad_x, "pipe", -1)
    outs = tuple((total.astype(jnp.bfloat16)[None] for total in totals))
    return (grad_x_all[None], outs[0], outs[1], outs[2], outs[3])


def solution(mesh):
    placed = (
        P(None, "feat"),
        P("pipe", None, "feat"),
        P("pipe", None, "feat"),
        P("pipe", None, "feat"),
        P("pipe", None, "feat"),
        P("pipe", "feat", None, None),
        P("pipe", "feat", None, None),
        P("pipe", "feat", None, None),
        P("pipe", "feat", None, None),
    )
    return jax.shard_map(
        shards,
        mesh=mesh,
        in_specs=placed,
        out_specs=(
            P("pipe", None, "feat"),
            P("pipe", "feat", None, None),
            P("pipe", "feat", None, None),
            P("pipe", "feat", None, None),
            P("pipe", "feat", None, None),
        ),
        check_vma=False,
    )
```

profile of v0, /device:TPU:40, one launch (start us, length us, event | category | flops | bytes accessed | tf_op | source)
XLA Modules:
  0.0 621.9 jit_solution(1889983177097769156)
XLA Ops:
  1.1 23.3 %all_to_all.160 = bf16[2,2,32,2,512]{4,3,1,0,2:T(2,128)(2,1)S(1)} all-to-all(bf16[2,2,32,2,512]{4,3,1,0,2:T(2,128)(2,1)S(1)} %copy.334), channel_id=1, replica_groups=mesh['pipe'=8,'feat'=32] {'feat'}, dimensions={2} | all-to-all | bytes 524288 | tf_op jit(solution)/shard_map/all_to_all | solution.py:49
  25.7 15.8 %all_to_all.161 = bf16[2,2,32,2,512]{4,3,1,0,2:T(2,128)(2,1)S(1)} all-to-all(bf16[2,2,32,2,512]{4,3,1,0,2:T(2,128)(2,1)S(1)} %copy.337), channel_id=1, replica_groups=mesh['pipe'=8,'feat'=32] {'feat'}, dimensions={2} | all-to-all | bytes 524288 | tf_op jit(solution)/shard_map/all_to_all | solution.py:54
  44.4 15.5 %all_to_all.162 = bf16[2,2,32,2,512]{4,3,1,0,2:T(2,128)(2,1)S(1)} all-to-all(bf16[2,2,32,2,512]{4,3,1,0,2:T(2,128)(2,1)S(1)} %copy.342), channel_id=1, replica_groups=mesh['pipe'=8,'feat'=32] {'feat'}, dimensions={2} | all-to-all | bytes 524288 | tf_op jit(solution)/shard_map/all_to_all | solution.py:63
  61.5 15.2 %all_to_all.163 = bf16[2,2,32,2,512]{4,3,1,0,2:T(2,128)(2,1)S(1)} all-to-all(bf16[2,2,32,2,512]{4,3,1,0,2:T(2,128)(2,1)S(1)} %copy.345), channel_id=1, replica_groups=mesh['pipe'=8,'feat'=32] {'feat'}, dimensions={2} | all-to-all | bytes 524288 | tf_op jit(solution)/shard_map/all_to_all | solution.py:68
  85.2 17.3 %all_to_all.164 = bf16[2,2,32,2,512]{4,3,1,0,2:T(2,128)(2,1)S(1)} all-to-all(bf16[2,2,32,2,512]{4,3,1,0,2:T(2,128)(2,1)S(1)} %copy.350), channel_id=1, replica_groups=mesh['pipe'=8,'feat'=32] {'feat'}, dimensions={2} | all-to-all | bytes 524288 | tf_op jit(solution)/shard_map/all_to_all | solution.py:49
  103.8 17.3 %all_to_all.165 = bf16[2,2,32,2,512]{4,3,1,0,2:T(2,128)(2,1)S(1)} all-to-all(bf16[2,2,32,2,512]{4,3,1,0,2:T(2,128)(2,1)S(1)} %copy.353), channel_id=1, replica_groups=mesh['pipe'=8,'feat'=32] {'feat'}, dimensions={2} | all-to-all | bytes 524288 | tf_op jit(solution)/shard_map/all_to_all | solution.py:54
  122.4 16.0 %all_to_all.166 = bf16[2,2,32,2,512]{4,3,1,0,2:T(2,128)(2,1)S(1)} all-to-all(bf16[2,2,32,2,512]{4,3,1,0,2:T(2,128)(2,1)S(1)} %copy.358), channel_id=1, replica_groups=mesh['pipe'=8,'feat'=32] {'feat'}, dimensions={2} | all-to-all | bytes 524288 | tf_op jit(solution)/shard_map/all_to_all | solution.py:63
  139.7 15.8 %all_to_all.167 = bf16[2,2,32,2,512]{4,3,1,0,2:T(2,128)(2,1)S(1)} all-to-all(bf16[2,2,32,2,512]{4,3,1,0,2:T(2,128)(2,1)S(1)} %copy.361), channel_id=1, replica_groups=mesh['pipe'=8,'feat'=32] {'feat'}, dimensions={2} | all-to-all | bytes 524288 | tf_op jit(solution)/shard_map/all_to_all | solution.py:68
  163.0 17.4 %all_to_all.168 = bf16[2,2,32,2,512]{4,3,1,0,2:T(2,128)(2,1)S(1)} all-to-all(bf16[2,2,32,2,512]{4,3,1,0,2:T(2,128)(2,1)S(1)} %copy.366), channel_id=1, replica_groups=mesh['pipe'=8,'feat'=32] {'feat'}, dimensions={2} | all-to-all | bytes 524288 | tf_op jit(solution)/shard_map/all_to_all | solution.py:49
  181.7 17.3 %all_to_all.169 = bf16[2,2,32,2,512]{4,3,1,0,2:T(2,128)(2,1)S(1)} all-to-all(bf16[2,2,32,2,512]{4,3,1,0,2:T(2,128)(2,1)S(1)} %copy.369), channel_id=1, replica_groups=mesh['pipe'=8,'feat'=32] {'feat'}, dimensions={2} | all-to-all | bytes 524288 | tf_op jit(solution)/shard_map/all_to_all | solution.py:54
  200.3 16.2 %all_to_all.170 = bf16[2,2,32,2,512]{4,3,1,0,2:T(2,128)(2,1)S(1)} all-to-all(bf16[2,2,32,2,512]{4,3,1,0,2:T(2,128)(2,1)S(1)} %copy.374), channel_id=1, replica_groups=mesh['pipe'=8,'feat'=32] {'feat'}, dimensions={2} | all-to-all | bytes 524288 | tf_op jit(solution)/shard_map/all_to_all | solution.py:63
  217.9 15.5 %all_to_all.171 = bf16[2,2,32,2,512]{4,3,1,0,2:T(2,128)(2,1)S(1)} all-to-all(bf16[2,2,32,2,512]{4,3,1,0,2:T(2,128)(2,1)S(1)} %copy.377), channel_id=1, replica_groups=mesh['pipe'=8,'feat'=32] {'feat'}, dimensions={2} | all-to-all | bytes 524288 | tf_op jit(solution)/shard_map/all_to_all | solution.py:68
  241.0 17.8 %all_to_all.172 = bf16[2,2,32,2,512]{4,3,1,0,2:T(2,128)(2,1)S(1)} all-to-all(bf16[2,2,32,2,512]{4,3,1,0,2:T(2,128)(2,1)S(1)} %copy.382), channel_id=1, replica_groups=mesh['pipe'=8,'feat'=32] {'feat'}, dimensions={2} | all-to-all | bytes 524288 | tf_op jit(solution)/shard_map/all_to_all | solution.py:49
  260.1 17.0 %all_to_all.173 = bf16[2,2,32,2,512]{4,3,1,0,2:T(2,128)(2,1)S(1)} all-to-all(bf16[2,2,32,2,512]{4,3,1,0,2:T(2,128)(2,1)S(1)} %copy.385), channel_id=1, replica_groups=mesh['pipe'=8,'feat'=32] {'feat'}, dimensions={2} | all-to-all | bytes 524288 | tf_op jit(solution)/shard_map/all_to_all | solution.py:54
  278.4 15.9 %all_to_all.174 = bf16[2,2,32,2,512]{4,3,1,0,2:T(2,128)(2,1)S(1)} all-to-all(bf16[2,2,32,2,512]{4,3,1,0,2:T(2,128)(2,1)S(1)} %copy.390), channel_id=1, replica_groups=mesh['pipe'=8,'feat'=32] {'feat'}, dimensions={2} | all-to-all | bytes 524288 | tf_op jit(solution)/shard_map/all_to_all | solution.py:63
  295.7 15.7 %all_to_all.175 = bf16[2,2,32,2,512]{4,3,1,0,2:T(2,128)(2,1)S(1)} all-to-all(bf16[2,2,32,2,512]{4,3,1,0,2:T(2,128)(2,1)S(1)} %copy.393), channel_id=1, replica_groups=mesh['pipe'=8,'feat'=32] {'feat'}, dimensions={2} | all-to-all | bytes 524288 | tf_op jit(solution)/shard_map/all_to_all | solution.py:68
  319.6 16.9 %all_to_all.176 = bf16[2,2,32,2,512]{4,3,1,0,2:T(2,128)(2,1)S(1)} all-to-all(bf16[2,2,32,2,512]{4,3,1,0,2:T(2,128)(2,1)S(1)} %copy.398), channel_id=1, replica_groups=mesh['pipe'=8,'feat'=32] {'feat'}, dimensions={2} | all-to-all | bytes 524288 | tf_op jit(solution)/shard_map/all_to_all | solution.py:49
  337.8 15.8 %all_to_all.177 = bf16[2,2,32,2,512]{4,3,1,0,2:T(2,128)(2,1)S(1)} all-to-all(bf16[2,2,32,2,512]{4,3,1,0,2:T(2,128)(2,1)S(1)} %copy.401), channel_id=1, replica_groups=mesh['pipe'=8,'feat'=32] {'feat'}, dimensions={2} | all-to-all | bytes 524288 | tf_op jit(solution)/shard_map/all_to_all | solution.py:54
  354.9 15.5 %all_to_all.178 = bf16[2,2,32,2,512]{4,3,1,0,2:T(2,128)(2,1)S(1)} all-to-all(bf16[2,2,32,2,512]{4,3,1,0,2:T(2,128)(2,1)S(1)} %copy.406), channel_id=1, replica_groups=mesh['pipe'=8,'feat'=32] {'feat'}, dimensions={2} | all-to-all | bytes 524288 | tf_op jit(solution)/shard_map/all_to_all | solution.py:63
  371.7 15.2 %all_to_all.179 = bf16[2,2,32,2,512]{4,3,1,0,2:T(2,128)(2,1)S(1)} all-to-all(bf16[2,2,32,2,512]{4,3,1,0,2:T(2,128)(2,1)S(1)} %copy.409), channel_id=1, replica_groups=mesh['pipe'=8,'feat'=32] {'feat'}, dimensions={2} | all-to-all | bytes 524288 | tf_op jit(solution)/shard_map/all_to_all | solution.py:68
  395.9 15.3 %all_to_all.180 = bf16[2,2,32,2,512]{4,3,1,0,2:T(2,128)(2,1)S(1)} all-to-all(bf16[2,2,32,2,512]{4,3,1,0,2:T(2,128)(2,1)S(1)} %copy.414), channel_id=1, replica_groups=mesh['pipe'=8,'feat'=32] {'feat'}, dimensions={2} | all-to-all | bytes 524288 | tf_op jit(solution)/shard_map/all_to_all | solution.py:49
  412.5 15.2 %all_to_all.181 = bf16[2,2,32,2,512]{4,3,1,0,2:T(2,128)(2,1)S(1)} all-to-all(bf16[2,2,32,2,512]{4,3,1,0,2:T(2,128)(2,1)S(1)} %copy.417), channel_id=1, replica_groups=mesh['pipe'=8,'feat'=32] {'feat'}, dimensions={2} | all-to-all | bytes 524288 | tf_op jit(solution)/shard_map/all_to_all | solution.py:54
  434.4 10.8 %all-to-all-done.22 = bf16[2,2,32,2,512]{4,3,1,0,2:T(2,128)(2,1)S(1)} async-done(((bf16[2,2,32,2,512]{4,3,1,0,2:T(2,128)(2,1)}), bf16[2,2,32,2,512]{4,3,1,0,2:T(2,128)(2,1)S(1)}, u32[]{:S(2)}, u32[]{:S(2)}) %all-to-all-start.22) | async-done | bytes 262176 | tf_op jit(solution)/shard_map/all_to_all | solution.py:63
  456.6 6.1 all-to-all-done.23
  479.1 9.0 %all-to-all-done.24 = bf16[2,2,32,2,512]{4,3,1,0,2:T(2,128)(2,1)S(1)} async-done(((bf16[2,2,32,2,512]{4,3,1,0,2:T(2,128)(2,1)}), bf16[2,2,32,2,512]{4,3,1,0,2:T(2,128)(2,1)S(1)}, u32[]{:S(2)}, u32[]{:S(2)}) %all-to-all-start.24) | async-done | bytes 262176 | tf_op jit(solution)/shard_map/all_to_all | solution.py:49
  497.5 8.2 %all-to-all-done.25 = bf16[2,2,32,2,512]{4,3,1,0,2:T(2,128)(2,1)S(1)} async-done(((bf16[2,2,32,2,512]{4,3,1,0,2:T(2,128)(2,1)}), bf16[2,2,32,2,512]{4,3,1,0,2:T(2,128)(2,1)S(1)}, u32[]{:S(2)}, u32[]{:S(2)}) %all-to-all-start.25) | async-done | bytes 262176 | tf_op jit(solution)/shard_map/all_to_all | solution.py:54
  514.4 8.8 %all-to-all-done.26 = bf16[2,2,32,2,512]{4,3,1,0,2:T(2,128)(2,1)S(1)} async-done(((bf16[2,2,32,2,512]{4,3,1,0,2:T(2,128)(2,1)}), bf16[2,2,32,2,512]{4,3,1,0,2:T(2,128)(2,1)S(1)}, u32[]{:S(2)}, u32[]{:S(2)}) %all-to-all-start.26) | async-done | bytes 262176 | tf_op jit(solution)/shard_map/all_to_all | solution.py:63
  532.0 8.2 %all-to-all-done.27 = bf16[2,2,32,2,512]{4,3,1,0,2:T(2,128)(2,1)S(1)} async-done(((bf16[2,2,32,2,512]{4,3,1,0,2:T(2,128)(2,1)}), bf16[2,2,32,2,512]{4,3,1,0,2:T(2,128)(2,1)S(1)}, u32[]{:S(2)}, u32[]{:S(2)}) %all-to-all-start.27) | async-done | bytes 262176 | tf_op jit(solution)/shard_map/all_to_all | solution.py:68
  556.3 9.0 %all-to-all-done.28 = bf16[2,2,32,2,512]{4,3,1,0,2:T(2,128)(2,1)S(1)} async-done(((bf16[2,2,32,2,512]{4,3,1,0,2:T(2,128)(2,1)}), bf16[2,2,32,2,512]{4,3,1,0,2:T(2,128)(2,1)S(1)}, u32[]{:S(2)}, u32[]{:S(2)}) %all-to-all-start.28) | async-done | bytes 262176 | tf_op jit(solution)/shard_map/all_to_all | solution.py:49
  573.6 8.8 %all-to-all-done.29 = bf16[2,2,32,2,512]{4,3,1,0,2:T(2,128)(2,1)S(1)} async-done(((bf16[2,2,32,2,512]{4,3,1,0,2:T(2,128)(2,1)}), bf16[2,2,32,2,512]{4,3,1,0,2:T(2,128)(2,1)S(1)}, u32[]{:S(2)}, u32[]{:S(2)}) %all-to-all-start.29) | async-done | bytes 262176 | tf_op jit(solution)/shard_map/all_to_all | solution.py:54
  591.4 8.7 %all-to-all-done.30 = bf16[2,2,32,2,512]{4,3,1,0,2:T(2,128)(2,1)S(1)} async-done(((bf16[2,2,32,2,512]{4,3,1,0,2:T(2,128)(2,1)}), bf16[2,2,32,2,512]{4,3,1,0,2:T(2,128)(2,1)S(1)}, u32[]{:S(2)}, u32[]{:S(2)}) %all-to-all-start.30) | async-done | bytes 262176 | tf_op jit(solution)/shard_map/all_to_all | solution.py:63
  608.8 8.2 %all-to-all-done.31 = bf16[2,2,32,2,512]{4,3,1,0,2:T(2,128)(2,1)S(1)} async-done(((bf16[2,2,32,2,512]{4,3,1,0,2:T(2,128)(2,1)}), bf16[2,2,32,2,512]{4,3,1,0,2:T(2,128)(2,1)S(1)}, u32[]{:S(2)}, u32[]{:S(2)}) %all-to-all-start.31) | async-done | bytes 262176 | tf_op jit(solution)/shard_map/all_to_all | solution.py:68
  (461 shorter events, 170.2 us)
Async XLA Ops:
  0.6 24.1 %copy-start = (bf16[1,2,128,128]{3,2,1,0:T(8,128)(2,1)S(1)}, bf16[1,2,128,128]{3,2,1,0:T(8,128)(2,1)}, u32[]{:S(2)}) copy-start(bf16[1,2,128,128]{3,2,1,0:T(8,128)(2,1)} %param.17) | copy-start | bytes 196612
  79.0 6.0 copy-start.54
  79.0 5.8 collective-permute-start
  156.8 5.8 copy-start.56
  156.8 5.8 collective-permute-start.1
  234.7 5.8 copy-start.58
  234.7 5.8 collective-permute-start.2
  312.6 5.8 copy-start.60
  312.6 5.8 collective-permute-start.3
  388.9 5.8 copy-start.62
  388.9 5.8 collective-permute-start.4
  429.7 4.6 copy-start.5
  429.7 15.5 %all-to-all-start.22 = ((bf16[2,2,32,2,512]{4,3,1,0,2:T(2,128)(2,1)}), bf16[2,2,32,2,512]{4,3,1,0,2:T(2,128)(2,1)S(1)}, u32[]{:S(2)}, u32[]{:S(2)}) async-start(bf16[2,2,32,2,512]{4,3,1,0,2:T(2,128)(2,1)} %copy.422), calls=%async_computation.22 | async-start | bytes 524288 | tf_op jit(solution)/shard_map/all_to_all | solution.py:63
  447.2 15.5 %all-to-all-start.23 = ((bf16[2,2,32,2,512]{4,3,1,0,2:T(2,128)(2,1)}), bf16[2,2,32,2,512]{4,3,1,0,2:T(2,128)(2,1)S(1)}, u32[]{:S(2)}, u32[]{:S(2)}) async-start(bf16[2,2,32,2,512]{4,3,1,0,2:T(2,128)(2,1)} %copy.425), calls=%async_computation.23 | async-start | bytes 524288 | tf_op jit(solution)/shard_map/all_to_all | solution.py:68
  464.7 5.9 collective-permute-start.5
  472.4 4.6 copy-start.31
  472.4 4.6 copy-start.81
  472.4 15.7 %all-to-all-start.24 = ((bf16[2,2,32,2,512]{4,3,1,0,2:T(2,128)(2,1)}), bf16[2,2,32,2,512]{4,3,1,0,2:T(2,128)(2,1)S(1)}, u32[]{:S(2)}, u32[]{:S(2)}) async-start(bf16[2,2,32,2,512]{4,3,1,0,2:T(2,128)(2,1)} %copy.430), calls=%async_computation.24 | async-start | bytes 524288 | tf_op jit(solution)/shard_map/all_to_all | solution.py:49
  490.1 4.5 copy-start.9
  490.1 15.6 %all-to-all-start.25 = ((bf16[2,2,32,2,512]{4,3,1,0,2:T(2,128)(2,1)}), bf16[2,2,32,2,512]{4,3,1,0,2:T(2,128)(2,1)S(1)}, u32[]{:S(2)}, u32[]{:S(2)}) async-start(bf16[2,2,32,2,512]{4,3,1,0,2:T(2,128)(2,1)} %copy.433), calls=%async_computation.25 | async-start | bytes 524288 | tf_op jit(solution)/shard_map/all_to_all | solution.py:54
  507.6 4.5 copy-start.23
  507.6 4.6 copy-start.72
  507.6 15.5 %all-to-all-start.26 = ((bf16[2,2,32,2,512]{4,3,1,0,2:T(2,128)(2,1)}), bf16[2,2,32,2,512]{4,3,1,0,2:T(2,128)(2,1)S(1)}, u32[]{:S(2)}, u32[]{:S(2)}) async-start(bf16[2,2,32,2,512]{4,3,1,0,2:T(2,128)(2,1)} %copy.438), calls=%async_computation.26 | async-start | bytes 524288 | tf_op jit(solution)/shard_map/all_to_all | solution.py:63
  524.7 15.5 %all-to-all-start.27 = ((bf16[2,2,32,2,512]{4,3,1,0,2:T(2,128)(2,1)}), bf16[2,2,32,2,512]{4,3,1,0,2:T(2,128)(2,1)S(1)}, u32[]{:S(2)}, u32[]{:S(2)}) async-start(bf16[2,2,32,2,512]{4,3,1,0,2:T(2,128)(2,1)} %copy.441), calls=%async_computation.27 | async-start | bytes 524288 | tf_op jit(solution)/shard_map/all_to_all | solution.py:68
  542.0 5.9 collective-permute-start.6
  549.8 15.6 %all-to-all-start.28 = ((bf16[2,2,32,2,512]{4,3,1,0,2:T(2,128)(2,1)}), bf16[2,2,32,2,512]{4,3,1,0,2:T(2,128)(2,1)S(1)}, u32[]{:S(2)}, u32[]{:S(2)}) async-start(bf16[2,2,32,2,512]{4,3,1,0,2:T(2,128)(2,1)} %copy.446), calls=%async_computation.28 | async-start | bytes 524288 | tf_op jit(solution)/shard_map/all_to_all | solution.py:49
  566.9 4.5 copy-start.87
  566.9 4.5 copy-start.91
  566.9 15.6 %all-to-all-start.29 = ((bf16[2,2,32,2,512]{4,3,1,0,2:T(2,128)(2,1)}), bf16[2,2,32,2,512]{4,3,1,0,2:T(2,128)(2,1)S(1)}, u32[]{:S(2)}, u32[]{:S(2)}) async-start(bf16[2,2,32,2,512]{4,3,1,0,2:T(2,128)(2,1)} %copy.449), calls=%async_computation.29 | async-start | bytes 524288 | tf_op jit(solution)/shard_map/all_to_all | solution.py:54
  584.4 4.8 copy-start.84
  584.4 15.7 %all-to-all-start.30 = ((bf16[2,2,32,2,512]{4,3,1,0,2:T(2,128)(2,1)}), bf16[2,2,32,2,512]{4,3,1,0,2:T(2,128)(2,1)S(1)}, u32[]{:S(2)}, u32[]{:S(2)}) async-start(bf16[2,2,32,2,512]{4,3,1,0,2:T(2,128)(2,1)} %copy.454), calls=%async_computation.30 | async-start | bytes 524288 | tf_op jit(solution)/shard_map/all_to_all | solution.py:63
  601.6 15.5 %all-to-all-start.31 = ((bf16[2,2,32,2,512]{4,3,1,0,2:T(2,128)(2,1)}), bf16[2,2,32,2,512]{4,3,1,0,2:T(2,128)(2,1)S(1)}, u32[]{:S(2)}, u32[]{:S(2)}) async-start(bf16[2,2,32,2,512]{4,3,1,0,2:T(2,128)(2,1)} %copy.457), calls=%async_computation.31 | async-start | bytes 524288 | tf_op jit(solution)/shard_map/all_to_all | solution.py:68
  (79 other events, 90.4 us)
where the time goes:
time: 633 us; the launch traced here: 622 us
  blocking collectives  363 us (57%)
  waiting for transfers between devices  111 us (18%)
  local copies, waits for them, and re-layouts  62.5 us (10%)
  starting transfers between devices  59.3 us (9%)
  matrix products  20 us (3%)
    all_to_all x6, blocking collectives, layer_backward(): lax.all_to_all(to_wire(dy, nfeat), 'feat', split_axis=2, concat_axis=2, t...  108 us
    all_to_all x6, blocking collectives, layer_backward(): lax.all_to_all(to_wire(back2, nfeat), 'feat', split_axis=2, concat_axis=2...  98.5 us
    all_to_all x5, blocking collectives, layer_backward(): lax.all_to_all(to_wire(pre_grad, nfeat), 'feat', split_axis=2, concat_axi...  79.1 us
    all_to_all x5, blocking collectives, layer_backward(): lax.all_to_all(to_wire(back1, nfeat), 'feat', split_axis=2, concat_axis=2...  77.4 us
    unnamed x191, local copies, waits for them, and re-layouts  29.4 us
    all_to_all x3, waiting for transfers between devices, layer_backward(): lax.all_to_all(to_wire(pre_grad, nfeat), 'feat', split_axis=2, concat_axi...  28.3 us
    ppermute x7, waiting for transfers between devices, passed_along(): return lax.ppermute(block, axis, route)  25.3 us
    all_to_all x3, waiting for transfers between devices, layer_backward(): lax.all_to_all(to_wire(back1, nfeat), 'feat', split_axis=2, concat_axis=2...  22.5 us
  transfers between devices with their start and end apart: 17, of which 17 were waited for; matrix products, arithmetic and copies ran while one was open for 3% of the time, Pallas kernels for 0%

commit v1 on v0

v1 whole, which is shorter than its diff:
```python
import functools

import jax
import jax.numpy as jnp
from jax import lax
from jax.experimental import pallas as pl
from jax.experimental.pallas import tpu as pltpu
from jax.sharding import PartitionSpec as P

BS = 128
BF = jnp.bfloat16
F32 = jnp.float32


def permuted(src, dst, tok):
    nb = src.shape[0] // tok
    low = lax.broadcasted_iota(jnp.int32, (nb, BS), 1) < nb
    for t in range(0, tok, 2):
        a = src[pl.ds(t, nb, stride=tok), :]
        b = src[pl.ds(t + 1, nb, stride=tok), :]
        y = jnp.concatenate([a, b], axis=0).T
        top, bot = y[:nb], y[nb:]
        dst[pl.ds(t, nb, stride=tok), :] = jnp.where(low, top, pltpu.roll(bot, nb, 1))
        dst[pl.ds(t + 1, nb, stride=tok), :] = jnp.where(low, pltpu.roll(top, nb, 1), bot)


def section_kernel(
    active, dy_hbm, slope_hbm, w_hbm, e_old, e_hbm, gx_hbm,
    dy, slope, w, e, s1, s2, in_sem, w_sem, out_sem,
):
    nsrc, tok, width = dy.shape

    def lanes(k):
        return pl.ds(k * BS, BS)

    def rows(blk):
        return pl.ds(blk * tok, tok)

    @pl.when(active[0] == 1)
    def _():
        get_dy = pltpu.make_async_copy(dy_hbm, dy, in_sem.at[0])
        get_slope = pltpu.make_async_copy(slope_hbm, slope, in_sem.at[1])
        get_w = [
            pltpu.make_async_copy(w_hbm.at[:, pl.ds(2 * f, 2)], w.at[:, pl.ds(2 * f, 2)], w_sem.at[f])
            for f in range(4)
        ]
        put_e = [
            pltpu.make_async_copy(
                e.at[:, pl.ds(f * tok, tok)], e_hbm.at[:, pl.ds(f * tok, tok)], out_sem.at[f]
            )
            for f in range(5)
        ]
        put_gx = pltpu.make_async_copy(e.at[:, pl.ds(4 * tok, tok)], gx_hbm, out_sem.at[5])
        get_dy.start()
        get_w[0].start()
        get_w[1].start()
        get_slope.start()
        get_w[2].start()
        get_w[3].start()
        get_dy.wait()
        for s in range(nsrc):
            for k in range(2):
                s1[rows(2 * s + k), :] = dy[s, :, k * BS:(k + 1) * BS].astype(F32)
        for f in range(4):
            permuted(s1, s2, tok)
            get_w[f].wait()
            if f == 1:
                get_slope.wait()
            for s in range(nsrc):
                for k in range(2):
                    v = s2[rows(2 * s + k), :].astype(BF)
                    e[s, f * tok:(f + 1) * tok, k * BS:(k + 1) * BS] = v
                    out = jnp.dot(v, w[s, 2 * f + k], preferred_element_type=F32)
                    if f == 1:
                        out = out * slope[s, :, k * BS:(k + 1) * BS]
                    if f < 3:
                        s1[rows(2 * s + k), :] = out.astype(BF).astype(F32)
                    else:
                        out = out + dy[s, :, k * BS:(k + 1) * BS].astype(F32)
                        e[s, 4 * tok:5 * tok, k * BS:(k + 1) * BS] = out.astype(BF)
            put_e[f].start()
        put_gx.start()
        put_e[4].start()
        put_gx.wait()
        for f in range(5):
            put_e[f].wait()


def section(active, dy, slope, w, e):
    nsrc, tok, width = dy.shape
    anywhere = pl.BlockSpec(memory_space=pl.ANY)
    return pl.pallas_call(
        section_kernel,
        out_shape=(
            jax.ShapeDtypeStruct(e.shape, BF),
            jax.ShapeDtypeStruct(dy.shape, BF),
        ),
        in_specs=[pl.BlockSpec(memory_space=pltpu.SMEM)] + [anywhere] * 4,
        out_specs=(anywhere, anywhere),
        input_output_aliases={4: 0},
        scratch_shapes=[
            pltpu.VMEM(dy.shape, BF),
            pltpu.VMEM(slope.shape, F32),
            pltpu.VMEM(w.shape, BF),
            pltpu.VMEM(e.shape, BF),
            pltpu.VMEM((nsrc * 2 * tok, BS), F32),
            pltpu.VMEM((nsrc * 2 * tok, BS), F32),
            pltpu.SemaphoreType.DMA((2,)),
            pltpu.SemaphoreType.DMA((4,)),
            pltpu.SemaphoreType.DMA((6,)),
        ],
        compiler_params=pltpu.CompilerParams(vmem_limit_bytes=32 * 1024 * 1024),
        name="section",
    )(active, dy, slope, w, e)


def grads_kernel(tok, e, l2, r2, l1, r1, gx, g_r1, g_l1, g_r2, g_l2):
    nsrc = e.shape[0]
    for f, (left, out) in enumerate(((l2, g_l2), (r2, g_r2), (l1, g_l1), (r1, g_r1))):
        right = e[:, f * tok:(f + 1) * tok, :].reshape(nsrc * tok, -1)
        for k in range(2):
            cols = slice(k * BS, (k + 1) * BS)
            out[0, k] = lax.dot_general(
                left[0, :, cols], right[:, cols], (((0,), (0,)), ((), ())),
                preferred_element_type=F32,
            ).astype(BF)
    gx[0] = e[:, 4 * tok:5 * tok, :].reshape(nsrc * tok, -1)


def weight_grads(tok, e, l2, r2, l1, r1, w_shape):
    vmem = pl.BlockSpec(memory_space=pltpu.VMEM)
    return pl.pallas_call(
        functools.partial(grads_kernel, tok),
        out_shape=(jax.ShapeDtypeStruct(l2.shape, BF),)
        + tuple(jax.ShapeDtypeStruct(w_shape, BF) for _ in range(4)),
        in_specs=[vmem] * 5,
        out_specs=(vmem,) * 5,
        compiler_params=pltpu.CompilerParams(vmem_limit_bytes=32 * 1024 * 1024),
        name="weight_grads",
    )(e, l2, r2, l1, r1)


def shards(
    grad_out, saved_input, saved_first, saved_pre, saved_second,
    right_one, left_one, right_two, left_two,
):
    me = lax.axis_index("pipe")
    nsec = lax.axis_size("pipe")
    nfeat = lax.axis_size("feat")
    ntok, width = grad_out.shape
    tok = ntok // nfeat

    own = jnp.concatenate([left_two[0], right_two[0], left_one[0], right_one[0]], axis=0)
    own = jnp.swapaxes(own, 1, 2)
    w = lax.all_gather(own, "feat", axis=0, tiled=True).reshape(nfeat, 8, BS, BS)

    both = jnp.concatenate(
        [saved_pre[0].reshape(nfeat, tok, width), grad_out.reshape(nfeat, tok, width)], axis=1
    )
    both = lax.all_to_all(both, "feat", split_axis=0, concat_axis=0, tiled=True)
    z = both[:, :tok].astype(F32)
    dy = both[:, tok:]
    cdf = 0.5 * (1.0 + lax.erf(z * 0.7071067811865476))
    slope = cdf + z * jnp.exp(-0.5 * z * z) * 0.3989422804014327
    zf = saved_pre.astype(F32)
    act = (zf * (0.5 * (1.0 + lax.erf(zf * 0.7071067811865476)))).astype(BF)

    e = jnp.zeros((nfeat, 5 * tok, width), BF)
    for turn in range(nsec):
        sec = nsec - 1 - turn
        active = (me == sec).astype(jnp.int32).reshape(1)
        e, gx = section(active, dy, slope, w, e)
        if sec > 0:
            dy = lax.ppermute(gx, "pipe", [(sec, sec - 1)])
    e = lax.all_to_all(e, "feat", split_axis=0, concat_axis=0, tiled=True)
    return weight_grads(tok, e, saved_second, act, saved_first, saved_input, right_one.shape)


def solution(mesh):
    rows = P("pipe", None, "feat")
    blocks = P("pipe", "feat", None, None)
    return jax.shard_map(
        shards,
        mesh=mesh,
        in_specs=(P(None, "feat"),) + (rows,) * 4 + (blocks,) * 4,
        out_specs=(rows,) + (blocks,) * 4,
        check_vma=False,
    )
```

time: 633 us -> 269 us (0.42)
  the two profiles are of different devices: /device:TPU:40 before, /device:TPU:32 now
where the time goes in v1:
time: 269 us; the launch traced here: 268 us
  waiting for transfers between devices  186 us (69%)
  local copies, waits for them, and re-layouts  32.1 us (12%)
  starting transfers between devices  24.4 us (9%)
  between operations  14.4 us (5%)
  Pallas kernels  8.65 us (3%)
    ppermute x7, waiting for transfers between devices, shards(): dy = lax.ppermute(gx, 'pipe', [(sec, sec - 1)])  69.4 us
    all_gather x1, waiting for transfers between devices, shards(): lax.all_gather(own, 'feat', axis=0, tiled=True).reshape(nfeat, 8, BS, BS)  67.8 us
    unnamed x30, local copies, waits for them, and re-layouts  30.9 us
    all_to_all x1, waiting for transfers between devices, shards(): e = lax.all_to_all(e, 'feat', split_axis=0, concat_axis=0, tiled=True)  27.6 us
    all_to_all x1, waiting for transfers between devices, shards(): both = lax.all_to_all(both, 'feat', split_axis=0, concat_axis=0, tiled=True)  21.3 us
    all_to_all x1, starting transfers between devices, shards(): both = lax.all_to_all(both, 'feat', split_axis=0, concat_axis=0, tiled=True)  11.2 us
    all_to_all x1, starting transfers between devices, shards(): e = lax.all_to_all(e, 'feat', split_axis=0, concat_axis=0, tiled=True)  7.78 us
    pallas_call x8, Pallas kernels, section(): pl.pallas_call(section_kernel, out_shape=(jax.ShapeDtypeStruct(e.shape, B...  7.48 us
  transfers between devices with their start and end apart: 10, of which 4 were waited for; matrix products, arithmetic and copies ran while one was open for 0% of the time, Pallas kernels for 0%

profile of v1, /device:TPU:32, one launch (start us, length us, event | category | flops | bytes accessed | tf_op | source)
XLA Modules:
  0.0 267.7 jit_solution(10608065630774878764)
XLA Ops:
  7.2 1.0 copy.23
  8.2 1.0 copy.24
  9.2 1.0 copy.25
  10.2 1.0 copy.26
  11.1 0.7 maximum_bitcast_fusion
  11.9 0.9 pad_maximum_fusion
  12.8 11.2 %all-to-all-start = ((bf16[32,32,256]{2,1,0:T(8,128)(2,1)}), bf16[32,32,256]{2,1,0:T(8,128)(2,1)S(1)}, u32[]{:S(2)}, u32[]{:S(2)}) async-start(bf16[32,32,256]{2,1,0:T(8,128)(2,1)} %pad_maximum_fusion), calls=%async_computation | async-start | bytes 1048576 | tf_op jit(solution)/shard_map/all_to_all | solution.py:160
  24.0 21.3 %all-to-all-done = bf16[32,32,256]{2,1,0:T(8,128)(2,1)S(1)} async-done(((bf16[32,32,256]{2,1,0:T(8,128)(2,1)}), bf16[32,32,256]{2,1,0:T(8,128)(2,1)S(1)}, u32[]{:S(2)}, u32[]{:S(2)}) %all-to-all-start) | async-done | bytes 524320 | tf_op jit(solution)/shard_map/all_to_all | solution.py:160
  45.4 0.2 fusion.7.slope_hbm
  45.6 67.8 %all-gather.2.cloned.1.call-done = bf16[256,128,128]{2,1,0:T(8,128)(2,1)} async-done(((bf16[8,128,128]{2,1,0:T(8,128)(2,1)}), bf16[256,128,128]{2,1,0:T(8,128)(2,1)}) %all-gather.2.cloned.1.call-update) | async-done | bytes 8388624 | tf_op jit(solution)/shard_map/all_gather | solution.py:155
  113.4 1.2 broadcast_in_dim.3.e_old
  114.6 3.4 %copy-done = bf16[256,128,128]{2,1,0:T(8,128)(2,1)S(1)} copy-done((bf16[256,128,128]{2,1,0:T(8,128)(2,1)S(1)}, bf16[256,128,128]{2,1,0:T(8,128)(2,1)}, u32[]{:S(2)}) %copy-start) | copy-done | bytes 8388632
  118.1 0.7 collective-permute-start
  118.8 3.4 %copy-done.1 = bf16[256,128,128]{2,1,0:T(8,128)(2,1)S(1)} copy-done((bf16[256,128,128]{2,1,0:T(8,128)(2,1)S(1)}, bf16[256,128,128]{2,1,0:T(8,128)(2,1)}, u32[]{:S(2)}) %copy-start.1) | copy-done | bytes 8388632
  122.3 0.7 collective-permute-start.1
  123.0 3.4 %copy-done.2 = bf16[256,128,128]{2,1,0:T(8,128)(2,1)S(1)} copy-done((bf16[256,128,128]{2,1,0:T(8,128)(2,1)S(1)}, bf16[256,128,128]{2,1,0:T(8,128)(2,1)}, u32[]{:S(2)}) %copy-start.2) | copy-done | bytes 8388632
  126.5 0.7 collective-permute-start.2
  127.2 3.4 %copy-done.3 = bf16[256,128,128]{2,1,0:T(8,128)(2,1)S(1)} copy-done((bf16[256,128,128]{2,1,0:T(8,128)(2,1)S(1)}, bf16[256,128,128]{2,1,0:T(8,128)(2,1)}, u32[]{:S(2)}) %copy-start.3) | copy-done | bytes 8388632
  130.7 0.7 collective-permute-start.3
  131.4 3.4 %copy-done.4 = bf16[256,128,128]{2,1,0:T(8,128)(2,1)S(1)} copy-done((bf16[256,128,128]{2,1,0:T(8,128)(2,1)S(1)}, bf16[256,128,128]{2,1,0:T(8,128)(2,1)}, u32[]{:S(2)}) %copy-start.4) | copy-done | bytes 8388632
  134.9 0.7 collective-permute-start.4
  135.6 3.4 %copy-done.5 = bf16[256,128,128]{2,1,0:T(8,128)(2,1)S(1)} copy-done((bf16[256,128,128]{2,1,0:T(8,128)(2,1)S(1)}, bf16[256,128,128]{2,1,0:T(8,128)(2,1)}, u32[]{:S(2)}) %copy-start.5) | copy-done | bytes 8388632
  139.1 0.7 collective-permute-start.5
  139.8 3.4 %copy-done.6 = bf16[256,128,128]{2,1,0:T(8,128)(2,1)S(1)} copy-done((bf16[256,128,128]{2,1,0:T(8,128)(2,1)S(1)}, bf16[256,128,128]{2,1,0:T(8,128)(2,1)}, u32[]{:S(2)}) %copy-start.6) | copy-done | bytes 8388632
  143.3 1.3 collective-permute-start.6
  144.6 69.4 %collective-permute-done.6.dy_hbm = bf16[32,16,256]{2,1,0:T(8,128)(2,1)S(1)} collective-permute-done((bf16[32,16,256]{2,1,0:T(8,128)(2,1)S(1)}, bf16[32,16,256]{2,1,0:T(8,128)(2,1)S(1)}, u32[]{:S(2)}, u32[]{:S(2)}) %collective-permute-start.6) | collective-permute-done | bytes 262176 | tf_op jit(solution)/shard_map/ppermute | solution.py:174
  214.0 3.4 %copy-done.7 = bf16[256,128,128]{2,1,0:T(8,128)(2,1)S(1)} copy-done((bf16[256,128,128]{2,1,0:T(8,128)(2,1)S(1)}, bf16[256,128,128]{2,1,0:T(8,128)(2,1)}, u32[]{:S(2)}) %copy-start.7) | copy-done | bytes 8388632
  217.4 6.7 %section.15 = (bf16[32,80,256]{2,1,0:T(8,128)(2,1)}, bf16[32,16,256]{2,1,0:T(8,128)(2,1)}) custom-call(s32[1]{0:T(128)} %bitcast.active, bf16[32,16,256]{2,1,0:T(8,128)(2,1)S(1)} %collective-permute-done.6.dy_hbm, f32[32,16,256]{2,1,0:T(8,128)S(1)} %fusion.7.slope_hbm, bf16[32,8,128,128]{3,2,1,0:T(8,128)(2,1)S(1)} %bitcast.24, ...), custom_call_target="tpu_custom_call", output_to_operand_aliasing={{0}: (4, {})} | custom-call | tf_op jit(solution)/shard_map/section/pallas_call | solution.py:92
  224.1 7.8 %all-to-all-start.1 = ((bf16[32,80,256]{2,1,0:T(8,128)(2,1)}), bf16[32,80,256]{2,1,0:T(8,128)(2,1)S(1)}, u32[]{:S(2)}, u32[]{:S(2)}) async-start(bf16[32,80,256]{2,1,0:T(8,128)(2,1)} %get-tuple-element.34), calls=%async_computation.1 | async-start | bytes 2621440 | tf_op jit(solution)/shard_map/all_to_all | solution.py:175
  231.9 0.1 fusion.3.r2
  232.1 27.6 %all-to-all-done.1.e = bf16[32,80,256]{2,1,0:T(8,128)(2,1)S(1)} async-done(((bf16[32,80,256]{2,1,0:T(8,128)(2,1)}), bf16[32,80,256]{2,1,0:T(8,128)(2,1)S(1)}, u32[]{:S(2)}, u32[]{:S(2)}) %all-to-all-start.1) | async-done | bytes 1310752 | tf_op jit(solution)/shard_map/all_to_all | solution.py:175
  259.7 1.2 weight_grads.1
  (34 shorter events, 0.9 us)
Async XLA Ops:
  7.2 4.7 %copy-start.11 = (bf16[1,512,256]{2,1,0:T(8,128)(2,1)S(1)}, bf16[1,512,256]{2,1,0:T(8,128)(2,1)}, u32[]{:S(2)}) copy-start(bf16[1,512,256]{2,1,0:T(8,128)(2,1)} %param.12) | copy-start | bytes 786436
  7.2 4.7 %copy-start.12 = (bf16[512,256]{1,0:T(8,128)(2,1)S(1)}, bf16[512,256]{1,0:T(8,128)(2,1)}, u32[]{:S(2)}) copy-start(bf16[512,256]{1,0:T(8,128)(2,1)} %param.9) | copy-start | bytes 786436
  7.2 106.2 %all-gather.2.cloned.1.call-start = ((), (), s32[]{:S(2)}) async-start(), calls=%async_computation.2 | async-start | bytes 8650752 | tf_op jit(solution)/shard_map/all_gather | solution.py:155
  12.8 32.5 %all-to-all-start = ((bf16[32,32,256]{2,1,0:T(8,128)(2,1)}), bf16[32,32,256]{2,1,0:T(8,128)(2,1)S(1)}, u32[]{:S(2)}, u32[]{:S(2)}) async-start(bf16[32,32,256]{2,1,0:T(8,128)(2,1)} %pad_maximum_fusion), calls=%async_computation | async-start | bytes 1048576 | tf_op jit(solution)/shard_map/all_to_all | solution.py:160
  114.6 3.4 %copy-start = (bf16[256,128,128]{2,1,0:T(8,128)(2,1)S(1)}, bf16[256,128,128]{2,1,0:T(8,128)(2,1)}, u32[]{:S(2)}) copy-start(bf16[256,128,128]{2,1,0:T(8,128)(2,1)} %all-gather.2.cloned.1.call-done) | copy-start | bytes 25165828
  118.1 0.7 collective-permute-start
  118.8 3.4 %copy-start.1 = (bf16[256,128,128]{2,1,0:T(8,128)(2,1)S(1)}, bf16[256,128,128]{2,1,0:T(8,128)(2,1)}, u32[]{:S(2)}) copy-start(bf16[256,128,128]{2,1,0:T(8,128)(2,1)} %all-gather.2.cloned.1.call-done) | copy-start | bytes 25165828
  122.3 0.7 collective-permute-start.1
  123.0 3.4 %copy-start.2 = (bf16[256,128,128]{2,1,0:T(8,128)(2,1)S(1)}, bf16[256,128,128]{2,1,0:T(8,128)(2,1)}, u32[]{:S(2)}) copy-start(bf16[256,128,128]{2,1,0:T(8,128)(2,1)} %all-gather.2.cloned.1.call-done) | copy-start | bytes 25165828
  126.5 0.7 collective-permute-start.2
  127.2 3.4 %copy-start.3 = (bf16[256,128,128]{2,1,0:T(8,128)(2,1)S(1)}, bf16[256,128,128]{2,1,0:T(8,128)(2,1)}, u32[]{:S(2)}) copy-start(bf16[256,128,128]{2,1,0:T(8,128)(2,1)} %all-gather.2.cloned.1.call-done) | copy-start | bytes 25165828
  130.7 0.7 collective-permute-start.3
  131.4 3.4 %copy-start.4 = (bf16[256,128,128]{2,1,0:T(8,128)(2,1)S(1)}, bf16[256,128,128]{2,1,0:T(8,128)(2,1)}, u32[]{:S(2)}) copy-start(bf16[256,128,128]{2,1,0:T(8,128)(2,1)} %all-gather.2.cloned.1.call-done) | copy-start | bytes 25165828
  134.9 0.7 collective-permute-start.4
  135.6 3.4 %copy-start.5 = (bf16[256,128,128]{2,1,0:T(8,128)(2,1)S(1)}, bf16[256,128,128]{2,1,0:T(8,128)(2,1)}, u32[]{:S(2)}) copy-start(bf16[256,128,128]{2,1,0:T(8,128)(2,1)} %all-gather.2.cloned.1.call-done) | copy-start | bytes 25165828
  139.1 0.7 collective-permute-start.5
  139.8 3.4 %copy-start.6 = (bf16[256,128,128]{2,1,0:T(8,128)(2,1)S(1)}, bf16[256,128,128]{2,1,0:T(8,128)(2,1)}, u32[]{:S(2)}) copy-start(bf16[256,128,128]{2,1,0:T(8,128)(2,1)} %all-gather.2.cloned.1.call-done) | copy-start | bytes 25165828
  143.3 70.7 %collective-permute-start.6 = (bf16[32,16,256]{2,1,0:T(8,128)(2,1)S(1)}, bf16[32,16,256]{2,1,0:T(8,128)(2,1)S(1)}, u32[]{:S(2)}, u32[]{:S(2)}) collective-permute-start(bf16[32,16,256]{2,1,0:T(8,128)(2,1)S(1)} %get-tuple-element.32), channel_id=1, source_target_pairs={{32,0},{33,1},{34,2},{35,3},{36,4},{37,5},{38,6},{39,7},{40,8},{41... | collective-permute-start | bytes 786440 | tf_op jit(solution)/shard_map/ppermute | solution.py:174
  214.0 3.4 %copy-start.7 = (bf16[256,128,128]{2,1,0:T(8,128)(2,1)S(1)}, bf16[256,128,128]{2,1,0:T(8,128)(2,1)}, u32[]{:S(2)}) copy-start(bf16[256,128,128]{2,1,0:T(8,128)(2,1)} %all-gather.2.cloned.1.call-done) | copy-start | bytes 25165828
  224.1 35.6 %copy-start.8 = (bf16[1,512,256]{2,1,0:T(8,128)(2,1)S(1)}, bf16[1,512,256]{2,1,0:T(8,128)(2,1)}, u32[]{:S(2)}) copy-start(bf16[1,512,256]{2,1,0:T(8,128)(2,1)} %l2.1) | copy-start | bytes 786436
  224.1 35.6 %copy-start.9 = (bf16[1,512,256]{2,1,0:T(8,128)(2,1)S(1)}, bf16[1,512,256]{2,1,0:T(8,128)(2,1)}, u32[]{:S(2)}) copy-start(bf16[1,512,256]{2,1,0:T(8,128)(2,1)} %l1.1) | copy-start | bytes 786436
  224.1 35.6 %copy-start.10 = (bf16[1,512,256]{2,1,0:T(8,128)(2,1)S(1)}, bf16[1,512,256]{2,1,0:T(8,128)(2,1)}, u32[]{:S(2)}) copy-start(bf16[1,512,256]{2,1,0:T(8,128)(2,1)} %r1.1) | copy-start | bytes 786436
  224.1 35.6 %all-to-all-start.1 = ((bf16[32,80,256]{2,1,0:T(8,128)(2,1)}), bf16[32,80,256]{2,1,0:T(8,128)(2,1)S(1)}, u32[]{:S(2)}, u32[]{:S(2)}) async-start(bf16[32,80,256]{2,1,0:T(8,128)(2,1)} %get-tuple-element.34), calls=%async_computation.1 | async-start | bytes 2621440 | tf_op jit(solution)/shard_map/all_to_all | solution.py:175
Sparse Core Ops, SparseCore 0:
  12.0 101.3 all-gather.1

commit v2 on v1

--- a/solution.py
+++ b/solution.py
@@ -24,94 +24,76 @@
         dst[pl.ds(t + 1, nb, stride=tok), :] = jnp.where(low, pltpu.roll(top, nb, 1), bot)
 
 
-def section_kernel(
-    active, dy_hbm, slope_hbm, w_hbm, e_old, e_hbm, gx_hbm,
-    dy, slope, w, e, s1, s2, in_sem, w_sem, out_sem,
-):
+def section_kernel(again, active, dy, slope, w, *rest):
+    e, gx, s1, s2 = rest[1:] if again else rest
     nsrc, tok, width = dy.shape
-
-    def lanes(k):
-        return pl.ds(k * BS, BS)
 
     def rows(blk):
         return pl.ds(blk * tok, tok)
 
     @pl.when(active[0] == 1)
     def _():
-        get_dy = pltpu.make_async_copy(dy_hbm, dy, in_sem.at[0])
-        get_slope = pltpu.make_async_copy(slope_hbm, slope, in_sem.at[1])
-        get_w = [
-            pltpu.make_async_copy(w_hbm.at[:, pl.ds(2 * f, 2)], w.at[:, pl.ds(2 * f, 2)], w_sem.at[f])
-            for f in range(4)
-        ]
-        put_e = [
-            pltpu.make_async_copy(
-                e.at[:, pl.ds(f * tok, tok)], e_hbm.at[:, pl.ds(f * tok, tok)], out_sem.at[f]
-            )
-            for f in range(5)
-        ]
-        put_gx = pltpu.make_async_copy(e.at[:, pl.ds(4 * tok, tok)], gx_hbm, out_sem.at[5])
-        get_dy.start()
-        get_w[0].start()
-        get_w[1].start()
-        get_slope.start()
-        get_w[2].start()
-        get_w[3].start()
-        get_dy.wait()
+        first = lax.broadcasted_iota(jnp.int32, (tok, width), 1) < BS
+        zero = jnp.zeros((tok, width), BF)
         for s in range(nsrc):
             for k in range(2):
                 s1[rows(2 * s + k), :] = dy[s, :, k * BS:(k + 1) * BS].astype(F32)
         for f in range(4):
             permuted(s1, s2, tok)
-            get_w[f].wait()
-            if f == 1:
-                get_slope.wait()
             for s in range(nsrc):
-                for k in range(2):
-                    v = s2[rows(2 * s + k), :].astype(BF)
-                    e[s, f * tok:(f + 1) * tok, k * BS:(k + 1) * BS] = v
-                    out = jnp.dot(v, w[s, 2 * f + k], preferred_element_type=F32)
-                    if f == 1:
-                        out = out * slope[s, :, k * BS:(k + 1) * BS]
-                    if f < 3:
-                        s1[rows(2 * s + k), :] = out.astype(BF).astype(F32)
-                    else:
-                        out = out + dy[s, :, k * BS:(k + 1) * BS].astype(F32)
-                        e[s, 4 * tok:5 * tok, k * BS:(k + 1) * BS] = out.astype(BF)
-            put_e[f].start()
-        put_gx.start()
-        put_e[4].start()
-        put_gx.wait()
-        for f in range(5):
-            put_e[f].wait()
+                v = jnp.concatenate([s2[rows(2 * s), :].astype(BF), s2[rows(2 * s + 1), :].astype(BF)], axis=1)
+                e[s, f * tok:(f + 1) * tok, :] = v
+                pair = jnp.concatenate([jnp.where(first, v, zero), jnp.where(first, zero, v)], axis=0)
+                out = jnp.dot(pair, w[s, 2 * f:2 * f + 2].reshape(width, BS), preferred_element_type=F32)
+                if f == 1:
+                    out = out * jnp.concatenate([slope[s, :, :BS], slope[s, :, BS:]], axis=0)
+                if f < 3:
+                    s1[pl.ds(2 * s * tok, 2 * tok), :] = out.astype(BF).astype(F32)
+                else:
+                    out = jnp.concatenate([out[:tok], out[tok:]], axis=1)
+                    out = (out + dy[s].astype(F32)).astype(BF)
+                    e[s, 4 * tok:5 * tok, :] = out
+                    gx[s] = out
+
+
+def in_vmem(v):
+    return pltpu.with_memory_space_constraint(v, pltpu.VMEM)
 
 
 def section(active, dy, slope, w, e):
     nsrc, tok, width = dy.shape
-    anywhere = pl.BlockSpec(memory_space=pl.ANY)
+    smem = pl.BlockSpec(memory_space=pltpu.SMEM)
+    vmem = pl.BlockSpec(memory_space=pltpu.VMEM)
+    held = [in_vmem(dy), in_vmem(slope), in_vmem(w)]
+    if e is not None:
+        held.append(in_vmem(e))
     return pl.pallas_call(
-        section_kernel,
-        out_shape=(
-            jax.ShapeDtypeStruct(e.shape, BF),
-            jax.ShapeDtypeStruct(dy.shape, BF),
-        ),
-        in_specs=[pl.BlockSpec(memory_space=pltpu.SMEM)] + [anywhere] * 4,
-        out_specs=(anywhere, anywhere),
-        input_output_aliases={4: 0},
-        scratch_shapes=[
-            pltpu.VMEM(dy.shape, BF),
-            pltpu.VMEM(slope.shape, F32),
-            pltpu.VMEM(w.shape, BF),
-            pltpu.VMEM(e.shape, BF),
-            pltpu.VMEM((nsrc * 2 * tok, BS), F32),
-            pltpu.VMEM((nsrc * 2 * tok, BS), F32),
-            pltpu.SemaphoreType.DMA((2,)),
-            pltpu.SemaphoreType.DMA((4,)),
-            pltpu.SemaphoreType.DMA((6,)),
-        ],
-        compiler_params=pltpu.CompilerParams(vmem_limit_bytes=32 * 1024 * 1024),
+        functools.partial(section_kernel, e is not None),
+        out_shape=(pltpu.VMEM((nsrc, 5 * tok, width), BF), pltpu.VMEM(dy.shape, BF)),
+        in_specs=[smem] + [vmem] * len(held),
+        out_specs=(vmem, vmem),
+        input_output_aliases={} if e is None else {4: 0},
+        scratch_shapes=[pltpu.VMEM((nsrc * 2 * tok, BS), F32)] * 2,
+        compiler_params=pltpu.CompilerParams(vmem_limit_bytes=16 * 1024 * 1024),
         name="section",
-    )(active, dy, slope, w, e)
+    )(active, *held)
+
+
+def pack_kernel(l2, r2, l1, r1, out):
+    for f, w in enumerate((l2, r2, l1, r1)):
+        for k in range(2):
+            out[2 * f + k] = w[0, k].astype(F32).T.astype(BF)
+
+
+def pack(l2, r2, l1, r1):
+    vmem = pl.BlockSpec(memory_space=pltpu.VMEM)
+    return pl.pallas_call(
+        pack_kernel,
+        out_shape=jax.ShapeDtypeStruct((8, BS, BS), BF),
+        in_specs=[vmem] * 4,
+        out_specs=vmem,
+        name="pack",
+    )(l2, r2, l1, r1)
 
 
 def grads_kernel(tok, e, l2, r2, l1, r1, gx, g_r1, g_l1, g_r2, g_l2):
@@ -150,8 +132,7 @@
     ntok, width = grad_out.shape
     tok = ntok // nfeat
 
-    own = jnp.concatenate([left_two[0], right_two[0], left_one[0], right_one[0]], axis=0)
-    own = jnp.swapaxes(own, 1, 2)
+    own = pack(left_two, right_two, left_one, right_one)
     w = lax.all_gather(own, "feat", axis=0, tiled=True).reshape(nfeat, 8, BS, BS)
 
     both = jnp.concatenate(

time: 269 us -> 262 us (0.974)
  waiting for transfers between devices: 186 us -> 167 us
  Pallas kernels: 8.65 us -> 25.5 us
  local copies, waits for them, and re-layouts: 32.1 us -> 28.2 us
    ppermute x7, waiting for transfers between devices: 69.4 us -> 45.9 us  [shards(): dy = lax.ppermute(gx, 'pipe', [(sec, sec - 1)])]
    pallas_call x8 -> x9, Pallas kernels: 7.48 us -> 24.3 us  [the longest x8 22.5 us: section(): pl.pallas_call(functools.partial(section_kernel, e is not None), out_shap...]
    unnamed x30 -> x24, local copies, waits for them, and re-layouts: 30.9 us -> 27 us
    all_to_all x1, waiting for transfers between devices: 27.6 us -> 31.2 us  [shards(): e = lax.all_to_all(e, 'feat', split_axis=0, concat_axis=0, tiled=True)]
  transfers between devices with their start and end apart: 10 -> 10, of which waited for: 4 -> 4; matrix products, arithmetic and copies ran while one was open for 0% -> 1% of each run, Pallas kernels for 0% -> 0%
where the time goes in v2:
time: 262 us; the launch traced here: 261 us
  waiting for transfers between devices  167 us (64%)
  local copies, waits for them, and re-layouts  28.2 us (11%)
  Pallas kernels  25.5 us (10%)
  starting transfers between devices  24.3 us (9%)
  between operations  14.3 us (5%)
    all_gather x1, waiting for transfers between devices, shards(): lax.all_gather(own, 'feat', axis=0, tiled=True).reshape(nfeat, 8, BS, BS)  68.7 us
    ppermute x7, waiting for transfers between devices, shards(): dy = lax.ppermute(gx, 'pipe', [(sec, sec - 1)])  45.9 us
    all_to_all x1, waiting for transfers between devices, shards(): e = lax.all_to_all(e, 'feat', split_axis=0, concat_axis=0, tiled=True)  31.2 us
    unnamed x24, local copies, waits for them, and re-layouts  27 us
    pallas_call x8, Pallas kernels, section(): pl.pallas_call(functools.partial(section_kernel, e is not None), out_shap...  22.5 us
    all_to_all x1, waiting for transfers between devices, shards(): both = lax.all_to_all(both, 'feat', split_axis=0, concat_axis=0, tiled=True)  20.9 us
    all_to_all x1, starting transfers between devices, shards(): both = lax.all_to_all(both, 'feat', split_axis=0, concat_axis=0, tiled=True)  11.2 us
    all_to_all x1, starting transfers between devices, shards(): e = lax.all_to_all(e, 'feat', split_axis=0, concat_axis=0, tiled=True)  7.78 us
  transfers between devices with their start and end apart: 10, of which 4 were waited for; matrix products, arithmetic and copies ran while one was open for 1% of the time, Pallas kernels for 0%

profile of v2, /device:TPU:32, one launch (start us, length us, event | category | flops | bytes accessed | tf_op | source)
XLA Modules:
  0.0 261.2 jit_solution(5701863257192349149)
XLA Ops:
  7.2 1.8 pack.1
  9.0 1.9 pad_maximum_fusion
  10.9 11.2 %all-to-all-start = ((bf16[32,32,256]{2,1,0:T(8,128)(2,1)}), bf16[32,32,256]{2,1,0:T(8,128)(2,1)S(1)}, u32[]{:S(2)}, u32[]{:S(2)}) async-start(bf16[32,32,256]{2,1,0:T(8,128)(2,1)} %pad_maximum_fusion), calls=%async_computation | async-start | bytes 1048576 | tf_op jit(solution)/shard_map/all_to_all | solution.py:141
  22.1 20.9 %all-to-all-done = bf16[32,32,256]{2,1,0:T(8,128)(2,1)S(1)} async-done(((bf16[32,32,256]{2,1,0:T(8,128)(2,1)}), bf16[32,32,256]{2,1,0:T(8,128)(2,1)S(1)}, u32[]{:S(2)}, u32[]{:S(2)}) %all-to-all-start) | async-done | bytes 524320 | tf_op jit(solution)/shard_map/all_to_all | solution.py:141
  43.3 68.7 %all-gather.2.cloned.1.call-done = bf16[256,128,128]{2,1,0:T(8,128)(2,1)} async-done(((bf16[8,128,128]{2,1,0:T(8,128)(2,1)}), bf16[256,128,128]{2,1,0:T(8,128)(2,1)}) %all-gather.2.cloned.1.call-update) | async-done | bytes 8388624 | tf_op jit(solution)/shard_map/all_gather | solution.py:136
  112.0 1.2 broadcast_in_dim.3.rest_0_
  113.1 3.4 %copy-done = bf16[256,128,128]{2,1,0:T(8,128)(2,1)S(1)} copy-done((bf16[256,128,128]{2,1,0:T(8,128)(2,1)S(1)}, bf16[256,128,128]{2,1,0:T(8,128)(2,1)}, u32[]{:S(2)}) %copy-start) | copy-done | bytes 8388632
  116.5 2.4 section.8
  118.9 0.7 collective-permute-start
  119.6 3.4 %copy-done.1 = bf16[256,128,128]{2,1,0:T(8,128)(2,1)S(1)} copy-done((bf16[256,128,128]{2,1,0:T(8,128)(2,1)S(1)}, bf16[256,128,128]{2,1,0:T(8,128)(2,1)}, u32[]{:S(2)}) %copy-start.1) | copy-done | bytes 8388632
  123.0 2.4 section.9
  125.4 0.7 collective-permute-start.1
  126.1 3.4 %copy-done.2 = bf16[256,128,128]{2,1,0:T(8,128)(2,1)S(1)} copy-done((bf16[256,128,128]{2,1,0:T(8,128)(2,1)S(1)}, bf16[256,128,128]{2,1,0:T(8,128)(2,1)}, u32[]{:S(2)}) %copy-start.2) | copy-done | bytes 8388632
  129.5 2.4 section.10
  131.9 0.7 collective-permute-start.2
  132.6 3.4 %copy-done.3 = bf16[256,128,128]{2,1,0:T(8,128)(2,1)S(1)} copy-done((bf16[256,128,128]{2,1,0:T(8,128)(2,1)S(1)}, bf16[256,128,128]{2,1,0:T(8,128)(2,1)}, u32[]{:S(2)}) %copy-start.3) | copy-done | bytes 8388632
  136.0 2.4 section.11
  138.4 0.7 collective-permute-start.3
  139.1 3.4 %copy-done.4 = bf16[256,128,128]{2,1,0:T(8,128)(2,1)S(1)} copy-done((bf16[256,128,128]{2,1,0:T(8,128)(2,1)S(1)}, bf16[256,128,128]{2,1,0:T(8,128)(2,1)}, u32[]{:S(2)}) %copy-start.4) | copy-done | bytes 8388632
  142.5 2.4 section.12
  144.9 0.7 collective-permute-start.4
  145.6 3.4 %copy-done.5 = bf16[256,128,128]{2,1,0:T(8,128)(2,1)S(1)} copy-done((bf16[256,128,128]{2,1,0:T(8,128)(2,1)S(1)}, bf16[256,128,128]{2,1,0:T(8,128)(2,1)}, u32[]{:S(2)}) %copy-start.5) | copy-done | bytes 8388632
  149.0 2.4 section.13
  152.1 3.4 %copy-done.6 = bf16[256,128,128]{2,1,0:T(8,128)(2,1)S(1)} copy-done((bf16[256,128,128]{2,1,0:T(8,128)(2,1)S(1)}, bf16[256,128,128]{2,1,0:T(8,128)(2,1)}, u32[]{:S(2)}) %copy-start.6) | copy-done | bytes 8388632
  155.5 2.4 section.14
  157.9 1.3 collective-permute-start.6
  159.2 45.9 %collective-permute-done.6.dy = bf16[32,16,256]{2,1,0:T(8,128)(2,1)S(1)} collective-permute-done((bf16[32,16,256]{2,1,0:T(8,128)(2,1)S(1)}, bf16[32,16,256]{2,1,0:T(8,128)(2,1)S(1)}, u32[]{:S(2)}, u32[]{:S(2)}) %collective-permute-start.6) | collective-permute-done | bytes 262176 | tf_op jit(solution)/shard_map/ppermute | solution.py:155
  205.1 3.4 %copy-done.7 = bf16[256,128,128]{2,1,0:T(8,128)(2,1)S(1)} copy-done((bf16[256,128,128]{2,1,0:T(8,128)(2,1)S(1)}, bf16[256,128,128]{2,1,0:T(8,128)(2,1)}, u32[]{:S(2)}) %copy-start.7) | copy-done | bytes 8388632
  208.4 5.6 %section.15 = (bf16[32,80,256]{2,1,0:T(8,128)(2,1)}, bf16[32,16,256]{2,1,0:T(8,128)(2,1)}) custom-call(s32[1]{0:T(128)} %bitcast.active, bf16[32,16,256]{2,1,0:T(8,128)(2,1)S(1)} %collective-permute-done.6.dy, f32[32,16,256]{2,1,0:T(8,128)S(1)} %fusion.7.slope, bf16[32,8,128,128]{3,2,1,0:T(8,128)(2,1)S(1)} %bitcast.18, ...), custom_call_target="tpu_custom_call", output_to_operand_aliasing={{0}: (4, {})} | custom-call | tf_op jit(solution)/shard_map/section/pallas_call | solution.py:70
  214.1 7.8 %all-to-all-start.1 = ((bf16[32,80,256]{2,1,0:T(8,128)(2,1)}), bf16[32,80,256]{2,1,0:T(8,128)(2,1)S(1)}, u32[]{:S(2)}, u32[]{:S(2)}) async-start(bf16[32,80,256]{2,1,0:T(8,128)(2,1)} %get-tuple-element.34), calls=%async_computation.1 | async-start | bytes 2621440 | tf_op jit(solution)/shard_map/all_to_all | solution.py:156
  222.0 31.2 %all-to-all-done.1.e = bf16[32,80,256]{2,1,0:T(8,128)(2,1)S(1)} async-done(((bf16[32,80,256]{2,1,0:T(8,128)(2,1)}), bf16[32,80,256]{2,1,0:T(8,128)(2,1)S(1)}, u32[]{:S(2)}, u32[]{:S(2)}) %all-to-all-start.1) | async-done | bytes 1310752 | tf_op jit(solution)/shard_map/all_to_all | solution.py:156
  253.2 1.2 weight_grads.1
  (28 shorter events, 1.1 us)
Async XLA Ops:
  7.2 104.8 %all-gather.2.cloned.1.call-start = ((), (), s32[]{:S(2)}) async-start(), calls=%async_computation.2 | async-start | bytes 8650752 | tf_op jit(solution)/shard_map/all_gather | solution.py:136
  10.9 32.1 %all-to-all-start = ((bf16[32,32,256]{2,1,0:T(8,128)(2,1)}), bf16[32,32,256]{2,1,0:T(8,128)(2,1)S(1)}, u32[]{:S(2)}, u32[]{:S(2)}) async-start(bf16[32,32,256]{2,1,0:T(8,128)(2,1)} %pad_maximum_fusion), calls=%async_computation | async-start | bytes 1048576 | tf_op jit(solution)/shard_map/all_to_all | solution.py:141
  113.1 3.4 %copy-start = (bf16[256,128,128]{2,1,0:T(8,128)(2,1)S(1)}, bf16[256,128,128]{2,1,0:T(8,128)(2,1)}, u32[]{:S(2)}) copy-start(bf16[256,128,128]{2,1,0:T(8,128)(2,1)} %all-gather.2.cloned.1.call-done) | copy-start | bytes 25165828
  118.9 0.7 collective-permute-start
  119.6 3.4 %copy-start.1 = (bf16[256,128,128]{2,1,0:T(8,128)(2,1)S(1)}, bf16[256,128,128]{2,1,0:T(8,128)(2,1)}, u32[]{:S(2)}) copy-start(bf16[256,128,128]{2,1,0:T(8,128)(2,1)} %all-gather.2.cloned.1.call-done) | copy-start | bytes 25165828
  125.4 0.7 collective-permute-start.1
  126.1 3.4 %copy-start.2 = (bf16[256,128,128]{2,1,0:T(8,128)(2,1)S(1)}, bf16[256,128,128]{2,1,0:T(8,128)(2,1)}, u32[]{:S(2)}) copy-start(bf16[256,128,128]{2,1,0:T(8,128)(2,1)} %all-gather.2.cloned.1.call-done) | copy-start | bytes 25165828
  131.9 0.7 collective-permute-start.2
  132.6 3.4 %copy-start.3 = (bf16[256,128,128]{2,1,0:T(8,128)(2,1)S(1)}, bf16[256,128,128]{2,1,0:T(8,128)(2,1)}, u32[]{:S(2)}) copy-start(bf16[256,128,128]{2,1,0:T(8,128)(2,1)} %all-gather.2.cloned.1.call-done) | copy-start | bytes 25165828
  138.4 0.7 collective-permute-start.3
  139.1 3.4 %copy-start.4 = (bf16[256,128,128]{2,1,0:T(8,128)(2,1)S(1)}, bf16[256,128,128]{2,1,0:T(8,128)(2,1)}, u32[]{:S(2)}) copy-start(bf16[256,128,128]{2,1,0:T(8,128)(2,1)} %all-gather.2.cloned.1.call-done) | copy-start | bytes 25165828
  144.9 0.7 collective-permute-start.4
  145.6 3.4 %copy-start.5 = (bf16[256,128,128]{2,1,0:T(8,128)(2,1)S(1)}, bf16[256,128,128]{2,1,0:T(8,128)(2,1)}, u32[]{:S(2)}) copy-start(bf16[256,128,128]{2,1,0:T(8,128)(2,1)} %all-gather.2.cloned.1.call-done) | copy-start | bytes 25165828
  151.4 0.7 collective-permute-start.5
  152.1 3.4 %copy-start.6 = (bf16[256,128,128]{2,1,0:T(8,128)(2,1)S(1)}, bf16[256,128,128]{2,1,0:T(8,128)(2,1)}, u32[]{:S(2)}) copy-start(bf16[256,128,128]{2,1,0:T(8,128)(2,1)} %all-gather.2.cloned.1.call-done) | copy-start | bytes 25165828
  157.9 47.2 %collective-permute-start.6 = (bf16[32,16,256]{2,1,0:T(8,128)(2,1)S(1)}, bf16[32,16,256]{2,1,0:T(8,128)(2,1)S(1)}, u32[]{:S(2)}, u32[]{:S(2)}) collective-permute-start(bf16[32,16,256]{2,1,0:T(8,128)(2,1)S(1)} %get-tuple-element.32), channel_id=1, source_target_pairs={{32,0},{33,1},{34,2},{35,3},{36,4},{37,5},{38,6},{39,7},{40,8},{41... | collective-permute-start | bytes 786440 | tf_op jit(solution)/shard_map/ppermute | solution.py:155
  205.1 3.4 %copy-start.7 = (bf16[256,128,128]{2,1,0:T(8,128)(2,1)S(1)}, bf16[256,128,128]{2,1,0:T(8,128)(2,1)}, u32[]{:S(2)}) copy-start(bf16[256,128,128]{2,1,0:T(8,128)(2,1)} %all-gather.2.cloned.1.call-done) | copy-start | bytes 25165828
  214.0 7.8 %copy-start.11 = (bf16[1,512,256]{2,1,0:T(8,128)(2,1)S(1)}, bf16[1,512,256]{2,1,0:T(8,128)(2,1)}, u32[]{:S(2)}) copy-start(bf16[1,512,256]{2,1,0:T(8,128)(2,1)} %param.12) | copy-start | bytes 786436
  214.0 39.1 %copy-start.8 = (bf16[1,512,256]{2,1,0:T(8,128)(2,1)S(1)}, bf16[1,512,256]{2,1,0:T(8,128)(2,1)}, u32[]{:S(2)}) copy-start(bf16[1,512,256]{2,1,0:T(8,128)(2,1)} %l2.3) | copy-start | bytes 786436
  214.0 39.1 %copy-start.9 = (bf16[1,512,256]{2,1,0:T(8,128)(2,1)S(1)}, bf16[1,512,256]{2,1,0:T(8,128)(2,1)}, u32[]{:S(2)}) copy-start(bf16[1,512,256]{2,1,0:T(8,128)(2,1)} %l1.3) | copy-start | bytes 786436
  214.0 39.1 %copy-start.10 = (bf16[1,512,256]{2,1,0:T(8,128)(2,1)S(1)}, bf16[1,512,256]{2,1,0:T(8,128)(2,1)}, u32[]{:S(2)}) copy-start(bf16[1,512,256]{2,1,0:T(8,128)(2,1)} %r1.3) | copy-start | bytes 786436
  214.1 39.1 %all-to-all-start.1 = ((bf16[32,80,256]{2,1,0:T(8,128)(2,1)}), bf16[32,80,256]{2,1,0:T(8,128)(2,1)S(1)}, u32[]{:S(2)}, u32[]{:S(2)}) async-start(bf16[32,80,256]{2,1,0:T(8,128)(2,1)} %get-tuple-element.34), calls=%async_computation.1 | async-start | bytes 2621440 | tf_op jit(solution)/shard_map/all_to_all | solution.py:156
Sparse Core Ops, SparseCore 0:
  11.2 100.7 all-gather.1

commit v3 on v2

--- a/solution.py
+++ b/solution.py
@@ -24,8 +24,11 @@
         dst[pl.ds(t + 1, nb, stride=tok), :] = jnp.where(low, pltpu.roll(top, nb, 1), bot)
 
 
-def section_kernel(again, active, dy, slope, w, *rest):
-    e, gx, s1, s2 = rest[1:] if again else rest
+def section_kernel(last, active, dy, slope, w_hbm, e_old, *rest):
+    if last:
+        e_hbm, w, s1, s2, w_sems, e, sems = rest
+    else:
+        e, gx, w, s1, s2, w_sems = rest
     nsrc, tok, width = dy.shape
 
     def rows(blk):
@@ -33,6 +36,19 @@
 
     @pl.when(active[0] == 1)
     def _():
+        gets = [
+            pltpu.make_async_copy(w_hbm.at[:, pl.ds(2 * f, 2)], w.at[:, pl.ds(2 * f, 2)], w_sems.at[f])
+            for f in range(4)
+        ]
+        for get in gets:
+            get.start()
+        if last:
+            puts = [
+                pltpu.make_async_copy(
+                    e.at[:, pl.ds(f * tok, tok)], e_hbm.at[:, pl.ds(f * tok, tok)], sems.at[f]
+                )
+                for f in range(5)
+            ]
         first = lax.broadcasted_iota(jnp.int32, (tok, width), 1) < BS
         zero = jnp.zeros((tok, width), BF)
         for s in range(nsrc):
@@ -40,6 +56,7 @@
                 s1[rows(2 * s + k), :] = dy[s, :, k * BS:(k + 1) * BS].astype(F32)
         for f in range(4):
             permuted(s1, s2, tok)
+            gets[f].wait()
             for s in range(nsrc):
                 v = jnp.concatenate([s2[rows(2 * s), :].astype(BF), s2[rows(2 * s + 1), :].astype(BF)], axis=1)
                 e[s, f * tok:(f + 1) * tok, :] = v
@@ -53,30 +70,68 @@
                     out = jnp.concatenate([out[:tok], out[tok:]], axis=1)
                     out = (out + dy[s].astype(F32)).astype(BF)
                     e[s, 4 * tok:5 * tok, :] = out
-                    gx[s] = out
+                    if not last:
+                        gx[s] = out
+            if last:
+                puts[f].start()
+        if last:
+            puts[4].start()
+            for put in puts:
+                put.wait()
+
+    if last:
+        @pl.when(active[0] == 0)
+        def _():
+            put = pltpu.make_async_copy(e_old, e_hbm, sems.at[0])
+            put.start()
+            put.wait()
 
 
 def in_vmem(v):
     return pltpu.with_memory_space_constraint(v, pltpu.VMEM)
 
 
-def section(active, dy, slope, w, e):
+def section(active, dy, slope, w, e, last=False):
     nsrc, tok, width = dy.shape
     smem = pl.BlockSpec(memory_space=pltpu.SMEM)
     vmem = pl.BlockSpec(memory_space=pltpu.VMEM)
-    held = [in_vmem(dy), in_vmem(slope), in_vmem(w)]
-    if e is not None:
-        held.append(in_vmem(e))
-    return pl.pallas_call(
-        functools.partial(section_kernel, e is not None),
-        out_shape=(pltpu.VMEM((nsrc, 5 * tok, width), BF), pltpu.VMEM(dy.shape, BF)),
-        in_specs=[smem] + [vmem] * len(held),
-        out_specs=(vmem, vmem),
-        input_output_aliases={} if e is None else {4: 0},
-        scratch_shapes=[pltpu.VMEM((nsrc * 2 * tok, BS), F32)] * 2,
-        compiler_params=pltpu.CompilerParams(vmem_limit_bytes=16 * 1024 * 1024),
+    anywhere = pl.BlockSpec(memory_space=pl.ANY)
+    work = [
+        pltpu.VMEM(w.shape, BF),
+        pltpu.VMEM((nsrc * 2 * tok, BS), F32),
+        pltpu.VMEM((nsrc * 2 * tok, BS), F32),
+        pltpu.SemaphoreType.DMA((4,)),
+    ]
+    if last:
+        out_shape = jax.ShapeDtypeStruct(e.shape, BF)
+        out_specs, aliases = anywhere, {}
+        work += [pltpu.VMEM(e.shape, BF), pltpu.SemaphoreType.DMA((5,))]
+    else:
+        out_shape = (pltpu.VMEM(e.shape, BF), pltpu.VMEM(dy.shape, BF))
+        out_specs, aliases = (vmem, vmem), {4: 0}
+    return pl.pallas_call(
+        functools.partial(section_kernel, last),
+        out_shape=out_shape,
+        in_specs=[smem, vmem, vmem, anywhere, vmem],
+        out_specs=out_specs,
+        input_output_aliases=aliases,
+        scratch_shapes=work,
+        compiler_params=pltpu.CompilerParams(vmem_limit_bytes=20 * 1024 * 1024),
         name="section",
-    )(active, *held)
+    )(active, in_vmem(dy), in_vmem(slope), pltpu.with_memory_space_constraint(w, pltpu.HBM), in_vmem(e))
+
+
+def blank_kernel(e):
+    e[0] = jnp.zeros(e.shape[1:], BF)
+
+
+def blank(shape):
+    return pl.pallas_call(
+        blank_kernel,
+        out_shape=pltpu.VMEM(shape, BF),
+        out_specs=pl.BlockSpec(memory_space=pltpu.VMEM),
+        name="blank",
+    )()
 
 
 def pack_kernel(l2, r2, l1, r1, out):
@@ -146,13 +201,15 @@
     zf = saved_pre.astype(F32)
     act = (zf * (0.5 * (1.0 + lax.erf(zf * 0.7071067811865476)))).astype(BF)
 
-    e = jnp.zeros((nfeat, 5 * tok, width), BF)
+    e = blank((nfeat, 5 * tok, width))
     for turn in range(nsec):
         sec = nsec - 1 - turn
         active = (me == sec).astype(jnp.int32).reshape(1)
-        e, gx = section(active, dy, slope, w, e)
         if sec > 0:
+            e, gx = section(active, dy, slope, w, e)
             dy = lax.ppermute(gx, "pipe", [(sec, sec - 1)])
+        else:
+            e = section(active, dy, slope, w, e, last=True)
     e = lax.all_to_all(e, "feat", split_axis=0, concat_axis=0, tiled=True)
     return weight_grads(tok, e, saved_second, act, saved_first, saved_input, right_one.shape)
 

time: 262 us -> 228 us (0.87)
  local copies, waits for them, and re-layouts: 28.2 us -> 0.04 us
  Pallas kernels: 25.5 us -> 9.55 us
  waiting for transfers between devices: 167 us -> 177 us
    unnamed x24 -> x8, local copies, waits for them, and re-layouts: 27 us -> 0.03 us
    pallas_call x8 -> x9, Pallas kernels: 22.5 us -> 6.61 us  [the longest x8 6.6 us: section(): pl.pallas_call(functools.partial(section_kernel, last), out_shape=out_sha...]
    ppermute x7, waiting for transfers between devices: 45.9 us -> 57.9 us  [shards(): dy = lax.ppermute(gx, 'pipe', [(sec, sec - 1)])]
where the time goes in v3:
time: 228 us; the launch traced here: 227 us
  waiting for transfers between devices  177 us (78%)
  starting transfers between devices  24.4 us (11%)
  between operations  14.3 us (6%)
  Pallas kernels  9.55 us (4%)
  other arithmetic  2.3 us (1%)
    all_gather x1, waiting for transfers between devices, shards(): lax.all_gather(own, 'feat', axis=0, tiled=True).reshape(nfeat, 8, BS, BS)  68.6 us
    ppermute x7, waiting for transfers between devices, shards(): dy = lax.ppermute(gx, 'pipe', [(sec, sec - 1)])  57.9 us
    all_to_all x1, waiting for transfers between devices, shards(): e = lax.all_to_all(e, 'feat', split_axis=0, concat_axis=0, tiled=True)  29.3 us
    all_to_all x1, waiting for transfers between devices, shards(): both = lax.all_to_all(both, 'feat', split_axis=0, concat_axis=0, tiled=True)  20.9 us
    all_to_all x1, starting transfers between devices, shards(): both = lax.all_to_all(both, 'feat', split_axis=0, concat_axis=0, tiled=True)  11.2 us
    all_to_all x1, starting transfers between devices, shards(): e = lax.all_to_all(e, 'feat', split_axis=0, concat_axis=0, tiled=True)  7.77 us
    pallas_call x8, Pallas kernels, section(): pl.pallas_call(functools.partial(section_kernel, last), out_shape=out_sha...  6.6 us
    ppermute x7, starting transfers between devices, shards(): dy = lax.ppermute(gx, 'pipe', [(sec, sec - 1)])  5.36 us
  transfers between devices with their start and end apart: 10, of which 4 were waited for; matrix products, arithmetic and copies ran while one was open for 1% of the time, Pallas kernels for 0%

profile of v3, /device:TPU:32, one launch (start us, length us, event | category | flops | bytes accessed | tf_op | source)
XLA Modules:
  0.0 227.3 jit_solution(13966077680830970088)
XLA Ops:
  7.2 0.0 all-gather.2.cloned.1.call-start
  7.2 1.8 pack.1
  9.0 0.0 all-gather.2.cloned.1.call-update
  9.0 2.0 pad_maximum_fusion
  11.0 11.2 %all-to-all-start = ((bf16[32,32,256]{2,1,0:T(8,128)(2,1)}), bf16[32,32,256]{2,1,0:T(8,128)(2,1)S(1)}, u32[]{:S(2)}, u32[]{:S(2)}) async-start(bf16[32,32,256]{2,1,0:T(8,128)(2,1)} %pad_maximum_fusion), calls=%async_computation | async-start | bytes 1048576 | tf_op jit(solution)/shard_map/all_to_all | solution.py:196
  22.2 20.9 %all-to-all-done = bf16[32,32,256]{2,1,0:T(8,128)(2,1)S(1)} async-done(((bf16[32,32,256]{2,1,0:T(8,128)(2,1)}), bf16[32,32,256]{2,1,0:T(8,128)(2,1)S(1)}, u32[]{:S(2)}, u32[]{:S(2)}) %all-to-all-start) | async-done | bytes 524320 | tf_op jit(solution)/shard_map/all_to_all | solution.py:196
  43.1 0.2 fusion.7.slope
  43.3 68.6 %all-gather.2.cloned.1.call-done = bf16[256,128,128]{2,1,0:T(8,128)(2,1)} async-done(((bf16[8,128,128]{2,1,0:T(8,128)(2,1)}), bf16[256,128,128]{2,1,0:T(8,128)(2,1)}) %all-gather.2.cloned.1.call-update) | async-done | bytes 8388624 | tf_op jit(solution)/shard_map/all_gather | solution.py:191
  112.0 0.7 collective-permute-start
  112.7 0.0 collective-permute-done.dy
  112.7 0.7 collective-permute-start.1
  113.4 0.0 collective-permute-done.1.dy
  113.5 0.7 collective-permute-start.2
  114.2 0.0 collective-permute-done.2.dy
  114.2 0.2 section.11
  114.4 0.7 collective-permute-start.3
  115.1 0.0 collective-permute-done.3.dy
  115.2 0.7 collective-permute-start.4
  115.9 0.7 collective-permute-start.5
  116.6 0.0 collective-permute-done.5.dy
  116.6 0.3 section.14
  116.9 1.3 collective-permute-start.6
  118.2 57.8 %collective-permute-done.6.dy = bf16[32,16,256]{2,1,0:T(8,128)(2,1)S(1)} collective-permute-done((bf16[32,16,256]{2,1,0:T(8,128)(2,1)S(1)}, bf16[32,16,256]{2,1,0:T(8,128)(2,1)S(1)}, u32[]{:S(2)}, u32[]{:S(2)}) %collective-permute-start.6) | collective-permute-done | bytes 262176 | tf_op jit(solution)/shard_map/ppermute | solution.py:210
  176.1 5.9 %section.15 = bf16[32,80,256]{2,1,0:T(8,128)(2,1)} custom-call(s32[1]{0:T(128)} %bitcast.active, bf16[32,16,256]{2,1,0:T(8,128)(2,1)S(1)} %collective-permute-done.6.dy, f32[32,16,256]{2,1,0:T(8,128)S(1)} %fusion.7.slope, bf16[32,8,128,128]{3,2,1,0:T(8,128)(2,1)} %bitcast.18, bf16[32,80,256]{2,1,0:T(8,128)(2,1)S(1)} %get-tuple-element.32.e_old), custom_call_target="tpu_custom_call" | custom-call | tf_op jit(solution)/shard_map/section/pallas_call | solution.py:112
  182.0 0.0 copy-start.3
  182.0 0.0 copy-start
  182.0 0.0 copy-start.1
  182.0 0.0 copy-start.2
  182.0 7.8 %all-to-all-start.1 = ((bf16[32,80,256]{2,1,0:T(8,128)(2,1)}), bf16[32,80,256]{2,1,0:T(8,128)(2,1)S(1)}, u32[]{:S(2)}, u32[]{:S(2)}) async-start(bf16[32,80,256]{2,1,0:T(8,128)(2,1)} %section.15), calls=%async_computation.1 | async-start | bytes 2621440 | tf_op jit(solution)/shard_map/all_to_all | solution.py:213
  189.8 0.1 fusion.3.r2
  189.9 29.3 %all-to-all-done.1.e = bf16[32,80,256]{2,1,0:T(8,128)(2,1)S(1)} async-done(((bf16[32,80,256]{2,1,0:T(8,128)(2,1)}), bf16[32,80,256]{2,1,0:T(8,128)(2,1)S(1)}, u32[]{:S(2)}, u32[]{:S(2)}) %all-to-all-start.1) | async-done | bytes 1310752 | tf_op jit(solution)/shard_map/all_to_all | solution.py:213
  219.3 1.2 weight_grads.1
  (12 shorter events, 0.2 us)
Async XLA Ops:
  7.2 104.8 %all-gather.2.cloned.1.call-start = ((), (), s32[]{:S(2)}) async-start(), calls=%async_computation.2 | async-start | bytes 8650752 | tf_op jit(solution)/shard_map/all_gather | solution.py:191
  11.0 32.1 %all-to-all-start = ((bf16[32,32,256]{2,1,0:T(8,128)(2,1)}), bf16[32,32,256]{2,1,0:T(8,128)(2,1)S(1)}, u32[]{:S(2)}, u32[]{:S(2)}) async-start(bf16[32,32,256]{2,1,0:T(8,128)(2,1)} %pad_maximum_fusion), calls=%async_computation | async-start | bytes 1048576 | tf_op jit(solution)/shard_map/all_to_all | solution.py:196
  112.0 0.7 collective-permute-start
  112.7 0.7 collective-permute-start.1
  113.5 0.7 collective-permute-start.2
  114.4 0.7 collective-permute-start.3
  115.2 0.7 collective-permute-start.4
  115.9 0.7 collective-permute-start.5
  116.9 59.1 %collective-permute-start.6 = (bf16[32,16,256]{2,1,0:T(8,128)(2,1)S(1)}, bf16[32,16,256]{2,1,0:T(8,128)(2,1)S(1)}, u32[]{:S(2)}, u32[]{:S(2)}) collective-permute-start(bf16[32,16,256]{2,1,0:T(8,128)(2,1)S(1)} %get-tuple-element.31), channel_id=1, source_target_pairs={{32,0},{33,1},{34,2},{35,3},{36,4},{37,5},{38,6},{39,7},{40,8},{41... | collective-permute-start | bytes 786440 | tf_op jit(solution)/shard_map/ppermute | solution.py:210
  182.0 7.8 %copy-start.3 = (bf16[1,512,256]{2,1,0:T(8,128)(2,1)S(1)}, bf16[1,512,256]{2,1,0:T(8,128)(2,1)}, u32[]{:S(2)}) copy-start(bf16[1,512,256]{2,1,0:T(8,128)(2,1)} %param.12) | copy-start | bytes 786436
  182.0 37.3 %copy-start = (bf16[1,512,256]{2,1,0:T(8,128)(2,1)S(1)}, bf16[1,512,256]{2,1,0:T(8,128)(2,1)}, u32[]{:S(2)}) copy-start(bf16[1,512,256]{2,1,0:T(8,128)(2,1)} %l2.3) | copy-start | bytes 786436
  182.0 37.3 %copy-start.1 = (bf16[1,512,256]{2,1,0:T(8,128)(2,1)S(1)}, bf16[1,512,256]{2,1,0:T(8,128)(2,1)}, u32[]{:S(2)}) copy-start(bf16[1,512,256]{2,1,0:T(8,128)(2,1)} %l1.3) | copy-start | bytes 786436
  182.0 37.3 %copy-start.2 = (bf16[1,512,256]{2,1,0:T(8,128)(2,1)S(1)}, bf16[1,512,256]{2,1,0:T(8,128)(2,1)}, u32[]{:S(2)}) copy-start(bf16[1,512,256]{2,1,0:T(8,128)(2,1)} %r1.3) | copy-start | bytes 786436
  182.0 37.3 %all-to-all-start.1 = ((bf16[32,80,256]{2,1,0:T(8,128)(2,1)}), bf16[32,80,256]{2,1,0:T(8,128)(2,1)S(1)}, u32[]{:S(2)}, u32[]{:S(2)}) async-start(bf16[32,80,256]{2,1,0:T(8,128)(2,1)} %section.15), calls=%async_computation.1 | async-start | bytes 2621440 | tf_op jit(solution)/shard_map/all_to_all | solution.py:213
Sparse Core Ops, SparseCore 0:
  11.2 100.7 all-gather.1
